TPU v7x, 256 devices: a whole 4x4x8 slice. The times are simulated.
256 devices in a mesh: tm: 16 (over x_hi, y, core), rows: 16 (over x_lo, z).
Axes of the slice: x: 4 (x_hi: 2, x_lo: 2; x = x_hi * 2 + x_lo), y: 4, z: 8, core: 2. Of those that a mesh axis runs over, the one named last changes fastest.
Arguments:
- snapshots: bfloat16 [32768, 32768], P('tm', 'rows'), may hold values from -6 to 6
- spod_modes: bfloat16 [64, 2, 4, 32768], P('tm', None, None, 'rows'), may hold values from -0.046875 to 0.046875
- freq_index: int32 [64], replicated, may hold values from 1 to 128, as said below
- seg_offsets: int32 [8192], P('tm'), may hold values from 0 to 2047, as said below
Outputs:
- coefficients: float32 [64, 2, 4, 8192], P('rows', None, None, 'tm')
Inputs may be any that keep to these rules, and one draw needn't show every extreme that they name: Frequency f is bin freq_index[f] of a segment of 256 snapshots; values may repeat. Segment n starts at snapshot (n // 512) * 2048 + seg_offsets[n]; snapshots past the last one count as zeros.
All inputs are finite; a program needn't handle non-finite values.
Results may differ from a plain program's by a relative error of at most 0.0003.
Values may be sent and summed in bfloat16 or wider, within the bound.
A program may use at most 64 MiB of HBM per device.

v0:
```python
import math
import jax
import jax.numpy as jnp
from jax import lax
from jax.sharding import PartitionSpec as P

F = 64
M = 4
L = 256


def hann_weights(distance):
    inside = (distance >= 0) & (distance < L)
    angles = distance.astype(jnp.float32) * (2.0 * math.pi / L)
    values = math.sqrt(8.0 / (3.0 * L)) * (0.5 - 0.5 * jnp.cos(angles))
    return jnp.where(inside, values, 0.0)


def phase_pair(frequency, moments):
    phase_bin = frequency[:, None] * moments[None, :] % L
    angles = phase_bin.astype(jnp.float32) * (2.0 * math.pi / L)
    return (jnp.cos(angles)[:, None, :], jnp.sin(angles)[:, None, :])


def demodulate(projected, frequency, moments):
    cosine, sine_part = phase_pair(frequency, moments)
    real_in = projected[:, 0]
    imag_in = projected[:, 1]
    real_out = cosine * real_in - sine_part * imag_in
    imag_out = -(sine_part * real_in + cosine * imag_in)
    return jnp.stack([real_out, imag_out], 1)


def body(snapshots, spod_modes, freq_index, seg_offsets):
    time_len = snapshots.shape[0]
    tm_pos = lax.axis_index("tm")
    row_pos = lax.axis_index("rows")
    block_rows = lax.all_gather(spod_modes, "tm", axis=0, tiled=True)
    flat_modes = block_rows.reshape(F * 2 * M, block_rows.shape[3])
    partial = lax.dot_general(
        flat_modes, snapshots, (((1,), (1,)), ((), ())), preferred_element_type=jnp.float32
    )
    route = [(i + 1, i) for i in range(lax.axis_size("tm") - 1)]
    behind = lax.ppermute(partial[:, :L], "tm", route)
    moments = tm_pos * time_len + jnp.arange(time_len + L, dtype=jnp.int32)

    def windowed(part, first, length):
        shaped = part.reshape(F, 2, M, length)
        demodulated = demodulate(shaped, freq_index, moments[first : first + length])
        at = first + jnp.arange(length, dtype=jnp.int32)
        weights = hann_weights(at[:, None] - seg_offsets[None, :])
        return lax.dot_general(
            demodulated.reshape(F * 2 * M, length),
            weights,
            (((1,), (0,)), ((), ())),
            precision=lax.Precision.HIGH,
            preferred_element_type=jnp.float32,
        )

    summed = windowed(partial, 0, time_len) + windowed(behind, time_len, L)
    summed = summed.reshape(F, 2, M, seg_offsets.shape[0])
    mine = lax.psum_scatter(summed, "rows", scatter_dimension=0, tiled=True)
    share_len = F // lax.axis_size("rows")
    own_freqs = lax.dynamic_slice_in_dim(freq_index, row_pos * share_len, share_len, 0)
    cosine, sine_part = phase_pair(own_freqs, tm_pos * time_len + seg_offsets)
    env_real = mine[:, 0]
    env_imag = mine[:, 1]
    return jnp.stack(
        [cosine * env_real - sine_part * env_imag, sine_part * env_real + cosine * env_imag], 1
    )


def solution(mesh):
    placed = (P("tm", "rows"), P("tm", None, None, "rows"), P(), P("tm"))
    return jax.shard_map(
        body, mesh=mesh, in_specs=placed, out_specs=P("rows", None, None, "tm"), check_vma=False
    )
```

profile of v0, /device:TPU:8, one launch (start us, length us, event | category | flops | bytes accessed | tf_op | source)
XLA Modules:
  0.0 268.1 jit_solution(8194953738576129666)
XLA Ops:
  6.5 0.7 all-gather.2.cloned.1.call-update
  7.3 0.0 all-reduce.3.cloned.1.call-start
  7.4 1.0 fusion.46
  8.4 2.8 %fusion.41 = (f32[64,2048]{1,0:T(8,128)S(1)}, f32[64,2048]{1,0:T(8,128)S(1)}) fusion(s32[2048]{0:T(1024)S(1)} %slice.36, s32[64]{0:T(128)} %param.6), kind=kLoop, calls=%fused_computation.53 | loop fusion | flops 1835008 | bytes 1057024 | tf_op jit(solution)/shard_map/cos | solution.py:22
  11.1 54.2 %all-gather.2.cloned.1.call-done = bf16[64,2,4,2048]{3,2,1,0:T(4,128)(2,1)} async-done(((bf16[4,2,4,2048]{3,2,1,0:T(4,128)(2,1)}), bf16[64,2,4,2048]{3,2,1,0:T(4,128)(2,1)}) %all-gather.2.cloned.1.call-update) | async-done | bytes 2097168 | tf_op jit(solution)/shard_map/all_gather | solution.py:38
  65.3 2.5 reshape.189
  67.8 7.0 %fusion.64 = f32[512,2048]{1,0:T(8,128)S(1)} fusion(bf16[512,2048]{1,0:T(8,128)(2,1)S(1)} %reshape.189, bf16[2048,2048]{1,0:T(8,128)(2,1)} %param.4), kind=kOutput, calls=%fused_computation.92 | convolution fusion | flops 4294967296 | bytes 14680064 | tf_op jit(solution)/shard_map/dot_general | solution.py:40
  74.8 1.9 copy-done
  76.8 5.2 %reshape.190 = f32[64,2,4,2048]{3,2,1,0:T(4,128)} reshape(f32[512,2048]{1,0:T(8,128)} %copy-done) | data formatting | bytes 8388608 | tf_op jit(solution)/shard_map/reshape | solution.py:48
  82.0 2.9 %multiply_subtract_fusion = (f32[64,1,4,2048]{3,2,1,0:T(4,128)S(1)}, f32[64,1,4,2048]{3,2,1,0:T(4,128)S(1)}) fusion(f32[64,2,4,2048]{3,2,1,0:T(4,128)} %reshape.190, f32[64,2048]{1,0:T(8,128)S(1)} %get-tuple-element.12, f32[64,2048]{1,0:T(8,128)S(1)} %get-tuple-element.11), kind=kLoop, calls=%fused_computation.21 | loop fusion | flops 3670016 | bytes 9437184 | tf_op jit(solution)/shard_map/sub | solution.py:29
  84.9 3.0 %pad_maximum_fusion = f32[64,2,4,2048]{3,2,1,0:T(4,128)} fusion(f32[64,1,4,2048]{3,2,1,0:T(4,128)S(1)} %get-tuple-element.6, f32[64,1,4,2048]{3,2,1,0:T(4,128)S(1)} %get-tuple-element.5), kind=kLoop, calls=%fused_computation | loop fusion | flops 1048576 | bytes 8388608 | tf_op jit(solution)/shard_map/stack | solution.py:31
  87.9 5.3 %reshape.191 = f32[512,2048]{1,0:T(8,128)} reshape(f32[64,2,4,2048]{3,2,1,0:T(4,128)} %pad_maximum_fusion) | data formatting | bytes 8388608 | tf_op jit(solution)/shard_map/reshape | solution.py:53
  93.2 2.8 %collective-permute-start = (f32[512,256]{1,0:T(8,128)S(1)}, f32[512,256]{1,0:T(8,128)S(1)}, u32[]{:S(2)}, u32[]{:S(2)}) collective-permute-start(f32[512,256]{1,0:T(8,128)S(1)} %slice.40), channel_id=1, source_target_pairs={{16,0},{32,16},{48,32},{64,48},{80,64},{96,80},{112,96},{128,112},... | collective-permute-start | bytes 1572872 | tf_op jit(solution)/shard_map/ppermute | solution.py:44
  96.0 20.9 %fusion = f32[512,512]{1,0:T(8,128)S(1)} fusion(f32[512,2048]{1,0:T(8,128)} %reshape.191, s32[512]{0:T(512)S(1)} %copy-done.1), kind=kOutput, calls=%fused_computation.1 | convolution fusion | flops 3231711232 | bytes 5244928 | tf_op jit(solution)/shard_map/dot_general | solution.py:52
  117.0 0.0 collective-permute-done
  117.0 0.1 reshape.192
  117.1 0.2 multiply_subtract_fusion.1
  117.3 0.0 copy-start.2
  117.3 0.0 copy-start.3
  117.3 0.1 pad_maximum_fusion.1
  117.4 0.2 reshape.193
  117.6 2.5 convolution_add_fusion
  120.1 1.3 reshape.194
  121.4 0.0 all-reduce.3.cloned.1.call-update
  121.5 0.0 copy-done.2
  121.5 0.1 dynamic_slice.3
  121.5 0.0 copy-done.3
  121.5 0.6 dynamic-slice
  122.8 0.2 fusion.51
  122.9 136.9 %all-reduce.3.cloned.1.call-done = f32[64,2,4,512]{3,2,1,0:T(4,128)} async-done(((f32[64,2,4,512]{3,2,1,0:T(4,128)}), f32[64,2,4,512]{3,2,1,0:T(4,128)}) %all-reduce.3.cloned.1.call-update) | async-done | bytes 1048592
  259.8 0.8 multiply_subtract_fusion.2
  260.6 0.6 pad_maximum_fusion.2
  (10 shorter events, 0.1 us)
Async XLA Ops:
  6.5 58.8 %all-gather.2.cloned.1.call-start = ((), (), s32[]{:S(2)}) async-start(), calls=%async_computation | async-start | bytes 2228224 | tf_op jit(solution)/shard_map/all_gather | solution.py:38
  7.3 252.6 %all-reduce.3.cloned.1.call-start = ((), (), s32[]{:S(2)}) async-start(), calls=%async_computation.1 | async-start | bytes 2097152
  74.8 1.9 copy-start
  87.9 8.1 %copy-start.1 = (s32[512]{0:T(512)S(1)}, s32[512]{0:T(512)}, u32[]{:S(2)}) copy-start(s32[512]{0:T(512)} %param.7) | copy-start | bytes 6148
  93.2 23.7 %collective-permute-start = (f32[512,256]{1,0:T(8,128)S(1)}, f32[512,256]{1,0:T(8,128)S(1)}, u32[]{:S(2)}, u32[]{:S(2)}) collective-permute-start(f32[512,256]{1,0:T(8,128)S(1)} %slice.40), channel_id=1, source_target_pairs={{16,0},{32,16},{48,32},{64,48},{80,64},{96,80},{112,96},{128,112},... | collective-permute-start | bytes 1572872 | tf_op jit(solution)/shard_map/ppermute | solution.py:44
  117.3 4.2 %copy-start.2 = (s32[64]{0:T(128)S(1)}, s32[64]{0:T(128)}, u32[]{:S(2)}) copy-start(s32[64]{0:T(128)} %param.6) | copy-start | bytes 772
  117.3 4.2 %copy-start.3 = (u32[256]{0:T(256)S(1)}, u32[256]{0:T(256)}, u32[]{:S(2)}) copy-start(u32[256]{0:T(256)} %constant.67) | copy-start | bytes 3076
Sparse Core Ops, SparseCore 0:
  10.1 55.1 all-gather.1
  121.6 138.2 all-reduce.2
where the time goes:
time: 269 us; the launch traced here: 268 us
  waiting for transfers between devices  192 us (71%)
  matrix products  30.4 us (11%)
  local copies, waits for them, and re-layouts  17.4 us (6%)
  between operations  14.3 us (5%)
  other arithmetic  11.5 us (4%)
  starting transfers between devices  2.82 us (1%)
    unnamed x3, waiting for transfers between devices  138 us
    all_gather x1, waiting for transfers between devices, body(): block_rows = lax.all_gather(spod_modes, 'tm', axis=0, tiled=True)  54.2 us
    dot_general x2, matrix products, windowed(): lax.dot_general(demodulated.reshape(F * 2 * M, length), weights, (((1,),...  23.4 us
    dot_general x1, matrix products, body(): lax.dot_general(flat_modes, snapshots, (((1,), (1,)), ((), ())), preferre...  6.96 us
    reshape x2, local copies, waits for them, and re-layouts, windowed(): demodulated.reshape(F * 2 * M, length)  5.51 us
  transfers between devices with their start and end apart: 3, of which 2 were waited for; matrix products, arithmetic and copies ran while one was open for 10% of the time, Pallas kernels for 0%

commit v1 on v0

--- a/solution.py
+++ b/solution.py
@@ -3,6 +3,7 @@
 import jax.numpy as jnp
 from jax import lax
 from jax.sharding import PartitionSpec as P
+from jax.lax import all_to_all, axis_size
 
 F = 64
 M = 4
@@ -35,7 +36,9 @@
     time_len = snapshots.shape[0]
     tm_pos = lax.axis_index("tm")
     row_pos = lax.axis_index("rows")
-    block_rows = lax.all_gather(spod_modes, "tm", axis=0, tiled=True)
+    block_rows = jnp.concatenate(
+        all_to_all(jnp.stack([spod_modes] * axis_size("tm")), "tm", 0, 0), axis=0
+    )
     flat_modes = block_rows.reshape(F * 2 * M, block_rows.shape[3])
     partial = lax.dot_general(
         flat_modes, snapshots, (((1,), (1,)), ((), ())), preferred_element_type=jnp.float32

time: 269 us -> 253 us (0.941)
  waiting for transfers between devices: 192 us -> 166 us
  starting transfers between devices: 2.82 us -> 10.8 us
  local copies, waits for them, and re-layouts: 17.4 us -> 20.1 us
    all_gather x1 -> x0, waiting for transfers between devices: 54.2 us -> none  [body(): block_rows = lax.all_gather(spod_modes, 'tm', axis=0, tiled=True)]
    all_to_all x0 -> x1, waiting for transfers between devices: none -> 24.7 us  [body(): all_to_all(jnp.stack([spod_modes] * axis_size('tm')), 'tm', 0, 0)]
    all_to_all x0 -> x1, starting transfers between devices: none -> 7.39 us  [body(): all_to_all(jnp.stack([spod_modes] * axis_size('tm')), 'tm', 0, 0)]
    another operation x0 -> x2, local copies, waits for them, and re-layouts: none -> 5.33 us  [the longest x1 3.29 us: body(): jnp.stack([spod_modes] * axis_size('tm'))]
    unnamed x3 -> x2, waiting for transfers between devices: 138 us -> 141 us
where the time goes in v1:
time: 253 us; the launch traced here: 252 us
  waiting for transfers between devices  166 us (66%)
  matrix products  31 us (12%)
  local copies, waits for them, and re-layouts  20.1 us (8%)
  between operations  14.2 us (6%)
  starting transfers between devices  10.8 us (4%)
  other arithmetic  10.2 us (4%)
    unnamed x2, waiting for transfers between devices  141 us
    all_to_all x1, waiting for transfers between devices, body(): all_to_all(jnp.stack([spod_modes] * axis_size('tm')), 'tm', 0, 0)  24.7 us
    dot_general x2, matrix products, windowed(): lax.dot_general(demodulated.reshape(F * 2 * M, length), weights, (((1,),...  23.4 us
    dot_general x1, matrix products, body(): lax.dot_general(flat_modes, snapshots, (((1,), (1,)), ((), ())), preferre...  7.63 us
    all_to_all x1, starting transfers between devices, body(): all_to_all(jnp.stack([spod_modes] * axis_size('tm')), 'tm', 0, 0)  7.39 us
    reshape x2, local copies, waits for them, and re-layouts, windowed(): demodulated.reshape(F * 2 * M, length)  5.5 us
    reshape x2, local copies, waits for them, and re-layouts, windowed(): shaped = part.reshape(F, 2, M, length)  5.34 us
  transfers between devices with their start and end apart: 3, of which 2 were waited for; matrix products, arithmetic and copies ran while one was open for 10% of the time, Pallas kernels for 0%

profile of v1, /device:TPU:8, one launch (start us, length us, event | category | flops | bytes accessed | tf_op | source)
XLA Modules:
  0.0 252.5 jit_solution(17369444606605512372)
XLA Ops:
  6.5 3.3 %stack.8 = bf16[16,4,2,4,2048]{4,3,2,1,0:T(4,128)(2,1)} broadcast(bf16[4,2,4,2048]{3,2,1,0:T(4,128)(2,1)} %param.5), dimensions={1,2,3,4} | broadcast | bytes 2228224 | tf_op jit(solution)/shard_map/stack | solution.py:40
  9.8 7.4 %all-to-all-start = ((bf16[16,4,2,4,2048]{4,3,2,1,0:T(4,128)(2,1)}), bf16[16,4,2,4,2048]{4,3,2,1,0:T(4,128)(2,1)S(1)}, u32[]{:S(2)}, u32[]{:S(2)}) async-start(bf16[16,4,2,4,2048]{4,3,2,1,0:T(4,128)(2,1)} %stack.8), calls=%async_computation | async-start | bytes 4194304 | tf_op jit(solution)/shard_map/all_to_all | solution.py:40
  17.2 0.0 all-reduce.3.cloned.1.call-start
  17.3 0.0 copy-done.2
  17.3 0.3 fusion.46
  17.7 2.1 fusion.41
  19.8 24.7 %all-to-all-done = bf16[16,4,2,4,2048]{4,3,2,1,0:T(4,128)(2,1)S(1)} async-done(((bf16[16,4,2,4,2048]{4,3,2,1,0:T(4,128)(2,1)}), bf16[16,4,2,4,2048]{4,3,2,1,0:T(4,128)(2,1)S(1)}, u32[]{:S(2)}, u32[]{:S(2)}) %all-to-all-start) | async-done | bytes 2097184 | tf_op jit(solution)/shard_map/all_to_all | solution.py:40
  44.5 2.0 reshape_reshape.3
  46.6 7.6 %fusion.64 = f32[512,2048]{1,0:T(8,128)S(1)} fusion(bf16[512,2048]{1,0:T(8,128)(2,1)} %reshape_reshape.3, bf16[2048,2048]{1,0:T(8,128)(2,1)} %param.4), kind=kOutput, calls=%fused_computation.92 | convolution fusion | flops 4294967296 | bytes 14680064 | tf_op jit(solution)/shard_map/dot_general | solution.py:43
  54.2 1.9 copy-done
  56.2 5.2 %reshape.188 = f32[64,2,4,2048]{3,2,1,0:T(4,128)} reshape(f32[512,2048]{1,0:T(8,128)} %copy-done) | data formatting | bytes 8388608 | tf_op jit(solution)/shard_map/reshape | solution.py:51
  61.4 2.9 %multiply_subtract_fusion = (f32[64,1,4,2048]{3,2,1,0:T(4,128)S(1)}, f32[64,1,4,2048]{3,2,1,0:T(4,128)S(1)}) fusion(f32[64,2,4,2048]{3,2,1,0:T(4,128)} %reshape.188, f32[64,2048]{1,0:T(8,128)S(1)} %get-tuple-element.12, f32[64,2048]{1,0:T(8,128)S(1)} %get-tuple-element.11), kind=kLoop, calls=%fused_computation.21 | loop fusion | flops 3670016 | bytes 9437184 | tf_op jit(solution)/shard_map/sub | solution.py:30
  64.2 3.0 %pad_maximum_fusion = f32[64,2,4,2048]{3,2,1,0:T(4,128)} fusion(f32[64,1,4,2048]{3,2,1,0:T(4,128)S(1)} %get-tuple-element.6, f32[64,1,4,2048]{3,2,1,0:T(4,128)S(1)} %get-tuple-element.5), kind=kLoop, calls=%fused_computation | loop fusion | flops 1048576 | bytes 8388608 | tf_op jit(solution)/shard_map/stack | solution.py:32
  67.3 5.3 %reshape.189 = f32[512,2048]{1,0:T(8,128)} reshape(f32[64,2,4,2048]{3,2,1,0:T(4,128)} %pad_maximum_fusion) | data formatting | bytes 8388608 | tf_op jit(solution)/shard_map/reshape | solution.py:56
  72.6 3.4 %collective-permute-start = (f32[512,256]{1,0:T(8,128)S(1)}, f32[512,256]{1,0:T(8,128)S(1)}, u32[]{:S(2)}, u32[]{:S(2)}) collective-permute-start(f32[512,256]{1,0:T(8,128)S(1)} %slice.40), channel_id=1, source_target_pairs={{16,0},{32,16},{48,32},{64,48},{80,64},{96,80},{112,96},{128,112},... | collective-permute-start | bytes 1572872 | tf_op jit(solution)/shard_map/ppermute | solution.py:47
  76.0 20.9 %fusion = f32[512,512]{1,0:T(8,128)S(1)} fusion(f32[512,2048]{1,0:T(8,128)} %reshape.189, s32[512]{0:T(512)S(1)} %copy-done.1), kind=kOutput, calls=%fused_computation.1 | convolution fusion | flops 3231711232 | bytes 5244928 | tf_op jit(solution)/shard_map/dot_general | solution.py:55
  96.9 0.0 collective-permute-done
  96.9 0.1 reshape.190
  97.1 0.2 multiply_subtract_fusion.1
  97.2 0.0 copy-start.3
  97.3 0.1 pad_maximum_fusion.1
  97.4 0.2 reshape.191
  97.6 2.5 convolution_add_fusion
  100.1 1.3 reshape.192
  101.4 0.0 all-reduce.3.cloned.1.call-update
  101.4 0.1 dynamic_slice.3
  101.5 0.0 copy-done.3
  101.5 0.6 dynamic-slice
  102.7 0.2 fusion.51
  102.9 141.3 %all-reduce.3.cloned.1.call-done = f32[64,2,4,512]{3,2,1,0:T(4,128)} async-done(((f32[64,2,4,512]{3,2,1,0:T(4,128)}), f32[64,2,4,512]{3,2,1,0:T(4,128)}) %all-reduce.3.cloned.1.call-update) | async-done | bytes 1048592
  244.2 0.8 multiply_subtract_fusion.2
  245.0 0.6 pad_maximum_fusion.2
  (10 shorter events, 0.1 us)
Async XLA Ops:
  6.5 10.8 %copy-start.2 = (s32[64]{0:T(128)S(1)}, s32[64]{0:T(128)}, u32[]{:S(2)}) copy-start(s32[64]{0:T(128)} %param.6) | copy-start | bytes 772
  9.8 34.7 %all-to-all-start = ((bf16[16,4,2,4,2048]{4,3,2,1,0:T(4,128)(2,1)}), bf16[16,4,2,4,2048]{4,3,2,1,0:T(4,128)(2,1)S(1)}, u32[]{:S(2)}, u32[]{:S(2)}) async-start(bf16[16,4,2,4,2048]{4,3,2,1,0:T(4,128)(2,1)} %stack.8), calls=%async_computation | async-start | bytes 4194304 | tf_op jit(solution)/shard_map/all_to_all | solution.py:40
  17.2 226.9 %all-reduce.3.cloned.1.call-start = ((), (), s32[]{:S(2)}) async-start(), calls=%async_computation.1 | async-start | bytes 2097152
  54.2 1.9 copy-start
  67.3 8.7 %copy-start.1 = (s32[512]{0:T(512)S(1)}, s32[512]{0:T(512)}, u32[]{:S(2)}) copy-start(s32[512]{0:T(512)} %param.7) | copy-start | bytes 6148
  72.6 24.3 %collective-permute-start = (f32[512,256]{1,0:T(8,128)S(1)}, f32[512,256]{1,0:T(8,128)S(1)}, u32[]{:S(2)}, u32[]{:S(2)}) collective-permute-start(f32[512,256]{1,0:T(8,128)S(1)} %slice.40), channel_id=1, source_target_pairs={{16,0},{32,16},{48,32},{64,48},{80,64},{96,80},{112,96},{128,112},... | collective-permute-start | bytes 1572872 | tf_op jit(solution)/shard_map/ppermute | solution.py:47
  97.2 4.2 %copy-start.3 = (u32[256]{0:T(256)S(1)}, u32[256]{0:T(256)}, u32[]{:S(2)}) copy-start(u32[256]{0:T(256)} %constant.67) | copy-start | bytes 3076
Sparse Core Ops, SparseCore 0:
  101.5 142.6 all-reduce.2
